TPU v7x, 512 devices: a whole 4x8x8 slice. The times are simulated.
512 devices in a mesh: section: 32 (over y, x), tp: 16 (over z, core).
Axes of the slice: x: 4, y: 8, z: 8, core: 2. Of those that a mesh axis runs over, the one named last changes fastest.
Arguments:
- leave_query: bfloat16 [32, 256, 4096], P('section', None, 'tp'), may hold values from -150 to 150
- leave_key: bfloat16 [32, 256, 4096], P('section', None, 'tp'), may hold values from -6 to 6
- leave_value: bfloat16 [32, 256, 4096], P('section', None, 'tp'), may hold values from -6 to 6
- arrive_query: bfloat16 [32, 256, 4096], P('section', None, 'tp'), may hold values from -150 to 150
- arrive_key: bfloat16 [32, 256, 4096], P('section', None, 'tp'), may hold values from -6 to 6
- arrive_value: bfloat16 [32, 256, 4096], P('section', None, 'tp'), may hold values from -6 to 6
- leave_residual: bfloat16 [32, 256, 6144], P('section', 'tp'), may hold values from -6 to 6
- out_weight: bfloat16 [32, 4096, 6144], P('section', 'tp'), may hold values from -0.5 to 0.5
- gate_scale: float32 [32, 6144], P('section'), may hold values from 0.25 to 1.75
- sign_bits: int32 [6144], replicated, may hold values 0 or 1
Outputs:
- arrived: bfloat16 [32, 256, 6144], P('section', 'tp')
All inputs are finite; a program needn't handle non-finite values.
Results may differ from a plain program's by a relative error of at most 0.0063.
Values may be sent and summed in bfloat16 or wider, within the bound.
A program may use at most 64 MiB of HBM per device.

v0:
```python
import math

import jax
import jax.numpy as jnp
from jax import lax
from jax.sharding import PartitionSpec as P

HD = 128
BLK = 128


def passed_along(x, axis, by):
    devices = lax.axis_size(axis)
    return lax.ppermute(x, axis, [(i, (i + by) % devices) for i in range(devices)])


def hadamard_matrix(order):
    index = jnp.arange(order, dtype=jnp.int32)
    anded = jnp.bitwise_and(index[:, None], index[None, :])
    parity = jnp.zeros((order, order), jnp.int32)
    for bit_number in range(order.bit_length() - 1):
        parity = parity + jnp.bitwise_and(jnp.right_shift(anded, bit_number), 1)
    signed = 1.0 - 2.0 * jnp.bitwise_and(parity, 1).astype(jnp.float32)
    return signed / math.sqrt(order)


def attend(query_rows, key_rows, value_rows):
    count = query_rows.shape[0]
    query_heads = query_rows.reshape(count, -1, HD)
    key_heads = key_rows.reshape(count, -1, HD)
    value_heads = value_rows.reshape(count, -1, HD)
    scores = jnp.einsum(
        "qhd,khd->hqk", query_heads, key_heads, preferred_element_type=jnp.float32
    ) / math.sqrt(HD)
    peak = jnp.max(scores, axis=-1, keepdims=True)
    raised = jnp.exp(scores - peak)
    probs = (raised / jnp.sum(raised, axis=-1, keepdims=True)).astype(jnp.bfloat16)
    mixed = jnp.einsum("hqk,khd->qhd", probs, value_heads, preferred_element_type=jnp.float32)
    return mixed.astype(jnp.bfloat16).reshape(count, -1)


def rotate(summed, hadamard_table, sign_row):
    row_count = summed.shape[0]
    blocks = summed.reshape(row_count, -1, BLK) * sign_row.reshape(-1, BLK)
    rotated = jnp.einsum("rnb,bc->rnc", blocks, hadamard_table, precision=lax.Precision.HIGHEST)
    return rotated.reshape(row_count, -1)


def add_sources(received):
    return jnp.sum(received.astype(jnp.float32), axis=0)


def local(
    leave_query,
    leave_key,
    leave_value,
    arrive_query,
    arrive_key,
    arrive_value,
    leave_residual,
    out_weight,
    gate_scale,
    sign_bits,
):
    groups = lax.axis_size("tp")
    hadamard_table = hadamard_matrix(BLK)
    sign_row = 1.0 - 2.0 * sign_bits.astype(jnp.float32)
    weight_rows = out_weight[0]
    gate_row = gate_scale[0]
    residual = leave_residual[0]
    share = residual.shape[0]
    width = residual.shape[1]

    def project(query_rows, key_rows, value_rows):
        attended = attend(query_rows[0], key_rows[0], value_rows[0])
        partial_value = (
            jnp.dot(attended, weight_rows, preferred_element_type=jnp.float32) * gate_row
        ).astype(jnp.bfloat16)
        return partial_value.reshape(groups, share, width)

    leave_partial = project(leave_query, leave_key, leave_value)
    arrive_partial = project(arrive_query, arrive_key, arrive_value)
    joint_partial = jnp.concatenate([leave_partial, arrive_partial], axis=1)
    totals = add_sources(
        lax.all_to_all(joint_partial, "tp", split_axis=0, concat_axis=0, tiled=True)
    )
    leave_total = totals[:share]
    arrive_total = totals[share:]
    leave_rotated = rotate(leave_total, hadamard_table, sign_row)
    handed = (residual.astype(jnp.float32) + leave_rotated).astype(jnp.bfloat16)
    passed = passed_along(handed, "section", 1)
    arrive_rotated = rotate(arrive_total, hadamard_table, sign_row)
    arrived = (passed.astype(jnp.float32) + arrive_rotated).astype(jnp.bfloat16)
    return arrived[None]


def solution(mesh):
    placed = (
        P("section", None, "tp"),
        P("section", None, "tp"),
        P("section", None, "tp"),
        P("section", None, "tp"),
        P("section", None, "tp"),
        P("section", None, "tp"),
        P("section", "tp", None),
        P("section", "tp", None),
        P("section", None),
        P(),
    )
    return jax.shard_map(
        local, mesh=mesh, in_specs=placed, out_specs=P("section", "tp", None), check_vma=False
    )
```

profile of v0, /device:TPU:1, one launch (start us, length us, event | category | flops | bytes accessed | tf_op | source)
XLA Modules:
  0.0 188.3 jit_solution(17493729584216696672)
XLA Ops:
  0.0 0.0 copy-start
  0.0 1.1 reshape_squeeze.18
  1.1 0.9 reshape_squeeze.19
  2.0 1.0 convolution_multiply_fusion.3
  3.1 0.3 fusion.58
  3.4 0.9 reshape_squeeze.21
  4.4 0.9 reshape_squeeze.22
  5.3 1.0 convolution_multiply_fusion.2
  6.3 0.3 fusion.53
  6.7 1.7 copy.21
  8.3 1.0 copy.22
  9.3 1.5 convolution_convert_fusion.1
  10.9 0.0 copy-done
  10.9 2.7 %fusion.2 = bf16[256,6144]{1,0:T(8,128)(2,1)} fusion(bf16[256,256]{0,1:T(8,128)(2,1)S(1)} %bitcast.62, bf16[1,256,6144]{2,1,0:T(8,128)(2,1)S(1)} %copy-done, f32[6144]{0:T(1024)S(1)} %bitcast.60), kind=kOutput, calls=%fused_computation.5 | convolution fusion | flops 808452096 | bytes 6447104 | tf_op jit(solution)/shard_map/dot_general | solution.py:77
  13.6 1.5 convolution_convert_fusion
  15.1 1.0 fusion.3
  16.1 0.9 copy-done.1
  16.9 3.4 %pad_maximum_fusion = bf16[16,32,6144]{2,1,0:T(8,128)(2,1)} fusion(bf16[16,16,6144]{2,1,0:T(8,128)(2,1)S(1)} %bitcast.57, bf16[16,16,6144]{2,1,0:T(8,128)(2,1)S(1)} %bitcast.56), kind=kLoop, calls=%fused_computation.7 | loop fusion | flops 12582912 | bytes 12582912 | tf_op jit(solution)/shard_map/concatenate | solution.py:83
  20.3 12.0 %all-to-all-start = ((bf16[16,32,6144]{2,1,0:T(8,128)(2,1)}), bf16[16,32,6144]{2,1,0:T(8,128)(2,1)}, u32[]{:S(2)}, u32[]{:S(2)}) async-start(bf16[16,32,6144]{2,1,0:T(8,128)(2,1)} %pad_maximum_fusion), calls=%async_computation | async-start | bytes 12582912 | tf_op jit(solution)/shard_map/all_to_all | solution.py:85
  32.3 0.0 copy-start.3
  32.4 138.5 %all-to-all-done = bf16[16,32,6144]{2,1,0:T(8,128)(2,1)} async-done(((bf16[16,32,6144]{2,1,0:T(8,128)(2,1)}), bf16[16,32,6144]{2,1,0:T(8,128)(2,1)}, u32[]{:S(2)}, u32[]{:S(2)}) %all-to-all-start) | async-done | bytes 6291488 | tf_op jit(solution)/shard_map/all_to_all | solution.py:85
  170.9 4.0 %convert_reduce_fusion = f32[32,6144]{1,0:T(8,128)S(1)} fusion(bf16[16,32,6144]{2,1,0:T(8,128)(2,1)} %all-to-all-done), kind=kLoop, calls=%fused_computation.2 | loop fusion | flops 6094848 | bytes 7077888 | tf_op jit(solution)/shard_map/reduce_sum | solution.py:50
  174.9 0.1 slice_bitcast_fusion.1
  174.9 0.1 copy.23
  175.0 0.1 copy.25
  175.1 0.1 bitcast_multiply_fusion.1
  175.2 0.5 fusion.19
  175.7 0.1 fusion.11
  175.9 3.1 %collective-permute-start = (bf16[16,6144]{1,0:T(8,128)(2,1)S(1)}, bf16[16,6144]{1,0:T(8,128)(2,1)S(1)}, u32[]{:S(2)}, u32[]{:S(2)}) collective-permute-start(bf16[16,6144]{1,0:T(8,128)(2,1)S(1)} %fusion.11), channel_id=1, source_target_pairs={{0,16},{16,32},{32,48},{48,64},{64,80},{80,96},{96,112},{112,128},... | collective-permute-start | bytes 589832 | tf_op jit(solution)/shard_map/ppermute | solution.py:14
  179.0 0.5 fusion.17
  179.5 8.0 %collective-permute-done = bf16[16,6144]{1,0:T(8,128)(2,1)S(1)} collective-permute-done((bf16[16,6144]{1,0:T(8,128)(2,1)S(1)}, bf16[16,6144]{1,0:T(8,128)(2,1)S(1)}, u32[]{:S(2)}, u32[]{:S(2)}) %collective-permute-start) | collective-permute-done | bytes 196640 | tf_op jit(solution)/shard_map/ppermute | solution.py:14
  187.5 0.8 fusion.12
  (7 shorter events, 0.0 us)
Async XLA Ops:
  0.0 10.9 %copy-start = (bf16[1,256,6144]{2,1,0:T(8,128)(2,1)S(1)}, bf16[1,256,6144]{2,1,0:T(8,128)(2,1)}, u32[]{:S(2)}) copy-start(bf16[1,256,6144]{2,1,0:T(8,128)(2,1)} %param.17) | copy-start | bytes 9437188
  0.0 10.9 %copy-start.2 = (f32[1,6144]{1,0:T(1,128)S(1)}, f32[1,6144]{1,0:T(1,128)}, u32[]{:S(2)}) copy-start(f32[1,6144]{1,0:T(1,128)} %param.18) | copy-start | bytes 73732
  15.1 1.9 %copy-start.1 = (bf16[256,6144]{1,0:T(8,128)(2,1)S(1)}, bf16[256,6144]{1,0:T(8,128)(2,1)}, u32[]{:S(2)}) copy-start(bf16[256,6144]{1,0:T(8,128)(2,1)} %fusion.2) | copy-start | bytes 9437188
  20.3 12.0 %copy-start.4 = (s32[6144]{0:T(1024)S(1)}, s32[6144]{0:T(1024)}, u32[]{:S(2)}) copy-start(s32[6144]{0:T(1024)} %param.19) | copy-start | bytes 73732
  20.3 150.5 %all-to-all-start = ((bf16[16,32,6144]{2,1,0:T(8,128)(2,1)}), bf16[16,32,6144]{2,1,0:T(8,128)(2,1)}, u32[]{:S(2)}, u32[]{:S(2)}) async-start(bf16[16,32,6144]{2,1,0:T(8,128)(2,1)} %pad_maximum_fusion), calls=%async_computation | async-start | bytes 12582912 | tf_op jit(solution)/shard_map/all_to_all | solution.py:85
  32.3 143.4 %copy-start.3 = (bf16[1,16,6144]{2,1,0:T(8,128)(2,1)S(1)}, bf16[1,16,6144]{2,1,0:T(8,128)(2,1)}, u32[]{:S(2)}) copy-start(bf16[1,16,6144]{2,1,0:T(8,128)(2,1)} %param.16) | copy-start | bytes 589828
  175.9 11.7 %collective-permute-start = (bf16[16,6144]{1,0:T(8,128)(2,1)S(1)}, bf16[16,6144]{1,0:T(8,128)(2,1)S(1)}, u32[]{:S(2)}, u32[]{:S(2)}) collective-permute-start(bf16[16,6144]{1,0:T(8,128)(2,1)S(1)} %fusion.11), channel_id=1, source_target_pairs={{0,16},{16,32},{32,48},{48,64},{64,80},{80,96},{96,112},{112,128},... | collective-permute-start | bytes 589832 | tf_op jit(solution)/shard_map/ppermute | solution.py:14
where the time goes:
time: 189 us; the launch traced here: 188 us
  waiting for transfers between devices  147 us (78%)
  starting transfers between devices  15.1 us (8%)
  matrix products  10.5 us (6%)
  other arithmetic  8.43 us (4%)
  local copies, waits for them, and re-layouts  7.68 us (4%)
    all_to_all x1, waiting for transfers between devices, local(): lax.all_to_all(joint_partial, 'tp', split_axis=0, concat_axis=0, tiled=True)  139 us
    all_to_all x1, starting transfers between devices, local(): lax.all_to_all(joint_partial, 'tp', split_axis=0, concat_axis=0, tiled=True)  12 us
    ppermute x1, waiting for transfers between devices, passed_along(): lax.ppermute(x, axis, [(i, (i + by) % devices) for i in range(devices)])  8.01 us
    reduce_sum x1, other arithmetic, add_sources(): return jnp.sum(received.astype(jnp.float32), axis=0)  4.02 us
  transfers between devices with their start and end apart: 2, of which 2 were waited for; matrix products, arithmetic and copies ran while one was open for 0% of the time, Pallas kernels for 0%

commit v1 on v0

v1 whole, which is shorter than its diff:
```python
import functools
import math

import jax
import jax.numpy as jnp
from jax import lax
from jax.experimental import pallas as pl
from jax.experimental.pallas import tpu as pltpu
from jax.sharding import PartitionSpec as P

HD = 128
BLK = 128
WIDE = 512
CHAINS = ((1, 4, 2), (-1, 3, 1))
MESH = pl.DeviceIdType.MESH
F32 = jnp.float32
BF16 = jnp.bfloat16


def kernel(
    lq, lk, lv, aq, ak, av, residual, weight, gate, sign_bits,
    out,
    qkv, qkv_sem,
    wbuf, w_sem, w_send, w_recv,
    att, att_send, att_recv,
    resbuf, res_sem, res_send, res_recv,
    table, signs, gates, gate_sem, sign_sem, bits_v,
    sums,
    zs, zr, zs_sem, zr_sem,
    xs, xr, xs_sem, xr_sem,
    fin, fs_sem, fin_sem,
    own0, own_keep, own_s, own_r, os_sem, or_sem,
    staged, out_sem,
):
    sections = lax.axis_size("section")
    chips = lax.axis_size("tp") // 2
    s = lax.axis_index("section")
    tp = lax.axis_index("tp")
    z = tp // 2
    c = tp % 2
    other = 1 - c
    tokens = lq.shape[1]
    kd = lq.shape[2]
    width = residual.shape[2]
    half = width // 2
    pieces = half // WIDE
    rows = tokens // chips
    mine = rows // 2

    next_section = {"section": lax.rem(s + 1, sections)}
    prev_section = {"section": lax.rem(s + sections - 1, sections)}
    partner = {"tp": 2 * z + other}

    def chip(at):
        return lax.rem(at + 2 * chips, chips)

    def turn(p, sign):
        return sign * (1 - 2 * lax.rem(p + c, 2))

    def cols(p, which):
        return pl.ds(pl.multiple_of(which * half + p * WIDE, 128), WIDE)

    loads = []
    for i, ref in enumerate((lq, lk, lv, aq, ak, av)):
        loads.append(pltpu.make_async_copy(ref.at[0], qkv.at[i], qkv_sem.at[i]))
        loads[-1].start()
    gate_copy = pltpu.make_async_copy(gate, gates, gate_sem)
    gate_copy.start()
    sign_copy = pltpu.make_async_copy(sign_bits, bits_v, sign_sem)
    sign_copy.start()

    def w_local(p):
        return pltpu.make_async_copy(weight.at[0, :, cols(p, c)], wbuf.at[p, pl.ds(0, kd)], w_sem.at[p])

    def w_remote(p):
        return pltpu.make_async_remote_copy(
            weight.at[0, :, cols(p, other)], wbuf.at[p, pl.ds(kd, kd)], w_send.at[p], w_recv.at[p],
            device_id=partner, device_id_type=MESH)

    def loop(body):
        lax.fori_loop(0, pieces, lambda p, _: (body(p), None)[1], None)

    loop(lambda p: w_local(p).start())
    own_rows = pl.ds(pl.multiple_of(mine * c, mine), mine)
    other_rows = pl.ds(pl.multiple_of(mine * other, mine), mine)
    res_local = pltpu.make_async_copy(
        residual.at[0, :, pl.ds(pl.multiple_of(c * half, 128), half)], resbuf.at[own_rows], res_sem)
    res_local.start()

    barrier = pltpu.get_barrier_semaphore()
    greeted = [partner, next_section, prev_section]
    for step in (1, -1):
        for core in (0, 1):
            greeted.append({"tp": 2 * chip(z + step) + core})
    for device in greeted:
        pl.semaphore_signal(barrier, inc=1, device_id=device, device_id_type=MESH)
    pl.semaphore_wait(barrier, len(greeted))

    loop(lambda p: w_remote(p).start())
    res_remote = pltpu.make_async_remote_copy(
        residual.at[0, :, pl.ds(pl.multiple_of(other * half, 128), half)], resbuf.at[own_rows], res_send, res_recv,
        device_id=partner, device_id_type=MESH)
    res_remote.start()

    def att_copy(m):
        there = att.at[pl.ds(m * tokens, tokens), pl.ds(kd, kd)]
        here = att.at[pl.ds(m * tokens, tokens), pl.ds(0, kd)]
        return pltpu.make_async_remote_copy(
            here, there, att_send.at[m], att_recv.at[m], device_id=partner, device_id_type=MESH)

    for m in range(2):
        for i in range(3):
            loads[3 * m + i].wait()
        for h in range(kd // HD):
            lanes = pl.ds(h * HD, HD)
            query, key, value = (qkv[3 * m + i, :, lanes] for i in range(3))
            scores = lax.dot_general(query, key, (((1,), (1,)), ((), ())), preferred_element_type=F32)
            scores = scores * (1.0 / math.sqrt(HD))
            peak = jnp.max(scores, axis=-1, keepdims=True)
            raised = jnp.exp(scores - peak)
            probs = (raised / jnp.sum(raised, axis=-1, keepdims=True)).astype(BF16)
            mixed = jnp.dot(probs, value, preferred_element_type=F32)
            att[pl.ds(m * tokens, tokens), lanes] = mixed.astype(BF16)
        att_copy(m).start()

    i = lax.broadcasted_iota(jnp.int32, (BLK, BLK), 0)
    j = lax.broadcasted_iota(jnp.int32, (BLK, BLK), 1)
    anded = i & j
    anded = anded ^ (anded >> 4)
    anded = anded ^ (anded >> 2)
    anded = anded ^ (anded >> 1)
    table[...] = (1 - 2 * (anded & 1)).astype(F32).astype(BF16)
    sign_copy.wait()
    signs[...] = 1.0 - 2.0 * bits_v[...].astype(F32)

    def turned(values):
        r = values.shape[0]
        blocks = jnp.concatenate([values[:, b * BLK:(b + 1) * BLK] for b in range(WIDE // BLK)], axis=0)
        made = jnp.dot(blocks, table[...], preferred_element_type=F32)
        return jnp.concatenate([made[b * r:(b + 1) * r] for b in range(WIDE // BLK)], axis=1)

    gate_copy.wait()
    res_local.wait()
    res_remote.wait_recv()
    for m in range(2):
        att_copy(m).wait_recv()

    def leaving(p, at):
        return sums[p, pl.ds(pl.multiple_of(rows * at, rows), rows), :]

    def arriving(p, at):
        return sums[p, pl.ds(pl.multiple_of(tokens + rows * at, rows), rows), :]

    def z_copy(ch, j, p):
        sign, _, _ = CHAINS[ch]
        to = {"tp": 2 * chip(z + turn(p, sign)) + c}
        return pltpu.make_async_remote_copy(
            zs[ch][j].at[p], zr[ch][j].at[p], zs_sem.at[ch, j, p], zr_sem.at[ch, j, p], device_id=to, device_id_type=MESH)

    def fin_copy(ch, core, p):
        sign, _, _ = CHAINS[ch]
        to = {"tp": 2 * chip(z + turn(p, sign)) + core}
        return pltpu.make_async_remote_copy(
            zs[ch][1].at[p, pl.ds(core * mine, mine)], fin.at[ch, c, p],
            fs_sem.at[ch, core, p], fin_sem.at[ch, c, p], device_id=to, device_id_type=MESH)

    def fin_arrival(ch, core, p):
        return pltpu.make_async_remote_copy(
            zs[ch][1].at[p, pl.ds(core * mine, mine)], fin.at[ch, core, p],
            fs_sem.at[ch, core, p], fin_sem.at[ch, core, p], device_id=partner, device_id_type=MESH)

    def x_copy(slot, p):
        return pltpu.make_async_remote_copy(
            xs.at[slot, p], xr.at[slot, p], xs_sem.at[slot, p], xr_sem.at[slot, p],
            device_id=next_section, device_id_type=MESH)

    def own_copy(p):
        return pltpu.make_async_remote_copy(
            own_s.at[p], own_r.at[p], os_sem.at[p], or_sem.at[p], device_id=partner, device_id_type=MESH)

    slots = {}
    for ch, (_, first, join) in enumerate(CHAINS):
        for j in range(1, join + 1):
            slots[ch, j] = len(slots) + 1

    def at(ch, j, p):
        return chip(z + j * turn(p, CHAINS[ch][0]))

    def apart(ch, j, p):
        first = CHAINS[ch][1]
        lead, tail = leaving(p, at(ch, j, p)), arriving(p, at(ch, j, p))
        if j < first:
            z_copy(ch, j + 1, p).wait_recv()
            lead = lead + zr[ch][j + 1][p, :rows].astype(F32)
            tail = tail + zr[ch][j + 1][p, rows:].astype(F32)
        zs[ch][j][p, :rows] = lead.astype(BF16)
        zs[ch][j][p, rows:] = tail.astype(BF16)
        z_copy(ch, j, p).start()

    def cross(ch, j, p):
        _, first, join = CHAINS[ch]
        lead = leaving(p, at(ch, j, p))
        if j == join and j < first:
            z_copy(ch, j + 1, p).wait_recv()
            lead = lead + zr[ch][j + 1][p, :rows].astype(F32)
        xs[slots[ch, j], p] = lead.astype(BF16)
        x_copy(slots[ch, j], p).start()

    def joined(ch, j, p):
        _, first, join = CHAINS[ch]
        x_copy(slots[ch, j], p).wait_recv()
        tail = arriving(p, at(ch, j, p)) + xr[slots[ch, j], p].astype(F32)
        if j < join:
            z_copy(ch, j + 1, p).wait_recv()
            tail = tail + zr[ch][j + 1][p].astype(F32)
        elif j < first:
            tail = tail + zr[ch][j + 1][p, rows:].astype(F32)
        zs[ch][j][p] = tail.astype(BF16)
        if j > 1:
            z_copy(ch, j, p).start()
        else:
            for core in (0, 1):
                fin_copy(ch, core, p).start()

    def own_cross(p):
        plain = turned(resbuf[:, pl.ds(pl.multiple_of(p * WIDE, 128), WIDE)])
        plain = plain * (signs[:, cols(p, c)] * (1.0 / math.sqrt(BLK)))
        xs[0, p] = (leaving(p, z) + plain).astype(BF16)
        x_copy(0, p).start()

    def own_joined(p):
        x_copy(0, p).wait_recv()
        own0[...] = arriving(p, z) + xr[0, p].astype(F32)
        own_keep[p] = own0[own_rows, :]
        own_s[p] = own0[other_rows, :].astype(BF16)
        own_copy(p).start()

    def project(p):
        w_local(p).wait()
        w_remote(p).wait_recv()
        made = jnp.dot(att[...], wbuf[p], preferred_element_type=F32)
        sums[p] = made * gates[:, cols(p, c)]

    def finish(core, p, own):
        for ch in range(len(CHAINS)):
            fin_arrival(ch, core, p).wait_recv()
        total = own + fin[0, core, p].astype(F32) + fin[1, core, p].astype(F32)
        total = total * signs[:, cols(p, core)]
        high = total.astype(BF16)
        low = (total - high.astype(F32)).astype(BF16)
        r = turned(jnp.concatenate([high, low], axis=0))
        r = (r[:mine] + r[mine:]) * (1.0 / math.sqrt(BLK))
        staged[core, p] = r.astype(BF16)
        out_copy(core, p).start()

    def out_copy(core, p):
        return pltpu.make_async_copy(staged.at[core, p], out.at[0, :, cols(p, core)], out_sem.at[core, p])

    def begin(p):
        project(p)
        for ch, (_, first, join) in enumerate(CHAINS):
            if first > join:
                apart(ch, first, p)
        own_cross(p)
        for ch, (_, first, join) in enumerate(CHAINS):
            for j in range(1, join + 1):
                if j < join or join == first:
                    cross(ch, j, p)

    loop(begin)
    most = max(first for _, first, _ in CHAINS)
    for back in range(1, most + 1):
        def middle(p, back=back):
            for ch, (_, first, join) in enumerate(CHAINS):
                j = first - back
                if j > join:
                    apart(ch, j, p)
                elif j == join:
                    cross(ch, j, p)

        def after(p, back=back):
            for ch, (_, first, join) in enumerate(CHAINS):
                j = first - back + 1
                if 1 <= j <= join:
                    joined(ch, j, p)

        loop(after)
        if any(first - back >= join for _, first, join in CHAINS):
            loop(middle)
        if back == most - 1:
            loop(own_joined)

    def finish_near(p):
        finish(c, p, own_keep[p])

    def finish_far(p):
        own_copy(p).wait_recv()
        finish(other, p, own_r[p].astype(F32))

    def finish_both(p):
        finish_near(p)
        finish_far(p)

    loop(finish_both)

    res_remote.wait_send()
    for m in range(2):
        att_copy(m).wait_send()

    def drain(p):
        w_remote(p).wait_send()
        for ch, (_, first, join) in enumerate(CHAINS):
            for j in range(2, first + 1):
                z_copy(ch, j, p).wait_send()
            for core in (0, 1):
                fin_copy(ch, core, p).wait_send()
        for slot in range(len(slots) + 1):
            x_copy(slot, p).wait_send()
        own_copy(p).wait_send()
        for core in (0, 1):
            out_copy(core, p).wait()

    loop(drain)


def local(
    leave_query, leave_key, leave_value, arrive_query, arrive_key, arrive_value,
    leave_residual, out_weight, gate_scale, sign_bits,
):
    tokens, kd = leave_query.shape[1:]
    width = leave_residual.shape[2]
    chips = lax.axis_size("tp") // 2
    rows, mine = tokens // chips, tokens // chips // 2
    half = width // 2
    pieces = half // WIDE
    dma = pltpu.SemaphoreType.DMA

    def hop_buffers():
        return [
            [None if j < 1 else pltpu.VMEM((pieces, 2 * rows if j > join else rows, WIDE), BF16)
             for j in range(first + 1)]
            for _, first, join in CHAINS
        ]

    def strip(tree):
        return [[pltpu.VMEM((1, 16, 128), BF16) if leaf is None else leaf for leaf in row] for row in tree]

    most = max(first for _, first, _ in CHAINS) + 1
    nx = 1 + sum(join for _, _, join in CHAINS)
    scratch = [
        pltpu.VMEM((6, tokens, kd), BF16), dma((6,)),
        pltpu.VMEM((pieces, 2 * kd, WIDE), BF16), dma((pieces,)), dma((pieces,)), dma((pieces,)),
        pltpu.VMEM((2 * tokens, 2 * kd), BF16), dma((2,)), dma((2,)),
        pltpu.VMEM((rows, half), BF16), dma, dma, dma,
        pltpu.VMEM((BLK, BLK), BF16), pltpu.VMEM((1, width), F32), pltpu.VMEM((1, width), F32), dma, dma,
        pltpu.VMEM((1, width), jnp.int32),
        pltpu.VMEM((pieces, 2 * tokens, WIDE), F32),
        strip(hop_buffers()), strip(hop_buffers()), dma((2, most, pieces)), dma((2, most, pieces)),
        pltpu.VMEM((nx, pieces, rows, WIDE), BF16), pltpu.VMEM((nx, pieces, rows, WIDE), BF16),
        dma((nx, pieces)), dma((nx, pieces)),
        pltpu.VMEM((2, 2, pieces, mine, WIDE), BF16), dma((2, 2, pieces)), dma((2, 2, pieces)),
        pltpu.VMEM((rows, WIDE), F32), pltpu.VMEM((pieces, mine, WIDE), F32),
        pltpu.VMEM((pieces, mine, WIDE), BF16), pltpu.VMEM((pieces, mine, WIDE), BF16),
        dma((pieces,)), dma((pieces,)),
        pltpu.VMEM((2, pieces, mine, WIDE), BF16), dma((2, pieces)),
    ]
    anywhere = pl.BlockSpec(memory_space=pltpu.HBM)
    return pl.pallas_call(
        kernel,
        out_shape=jax.ShapeDtypeStruct((1, mine, width), BF16),
        in_specs=[anywhere] * 10,
        out_specs=anywhere,
        scratch_shapes=scratch,
        compiler_params=pltpu.CompilerParams(
            collective_id=0, has_side_effects=True, vmem_limit_bytes=48 * 1024 * 1024),
        cost_estimate=pl.CostEstimate(
            flops=2 * 2 * tokens * kd * width, bytes_accessed=2 * kd * width, transcendentals=0),
    )(
        leave_query, leave_key, leave_value, arrive_query, arrive_key, arrive_value,
        leave_residual, out_weight, gate_scale, sign_bits.reshape(1, width),
    )


def solution(mesh):
    placed = (
        P("section", None, "tp"),
        P("section", None, "tp"),
        P("section", None, "tp"),
        P("section", None, "tp"),
        P("section", None, "tp"),
        P("section", None, "tp"),
        P("section", "tp", None),
        P("section", "tp", None),
        P("section", None),
        P(),
    )
    return jax.shard_map(
        local, mesh=mesh, in_specs=placed, out_specs=P("section", "tp", None), check_vma=False
    )
```

time: 189 us -> 63 us (0.33)
  waiting for transfers between devices: 147 us -> 0 us
  Pallas kernels: 0 us -> 52.2 us
  starting transfers between devices: 15.1 us -> 0 us
  matrix products: 10.5 us -> 0 us
  other arithmetic: 8.43 us -> 0 us
  local copies, waits for them, and re-layouts: 7.68 us -> 10.4 us
    all_to_all x1 -> x0, waiting for transfers between devices: 139 us -> none  [local(): lax.all_to_all(joint_partial, 'tp', split_axis=0, concat_axis=0, tiled=True)]
    pallas_call x0 -> x1, Pallas kernels: none -> 52.2 us  [local(): pl.pallas_call(kernel, out_shape=jax.ShapeDtypeStruct((1, mine, width), B...]
    all_to_all x1 -> x0, starting transfers between devices: 12 us -> none  [local(): lax.all_to_all(joint_partial, 'tp', split_axis=0, concat_axis=0, tiled=True)]
    dot_general x8 -> x0, matrix products: 9.77 us -> none  [the longest x2 3.68 us: project(): jnp.dot(attended, weight_rows, preferred_element_type=jnp.float32)]
    unnamed x13 -> x21, local copies, waits for them, and re-layouts: 1.1 us -> 10.4 us
    ppermute x1 -> x0, waiting for transfers between devices: 8.01 us -> none  [passed_along(): lax.ppermute(x, axis, [(i, (i + by) % devices) for i in range(devices)])]
    another operation x6 -> x0, local copies, waits for them, and re-layouts: 6.58 us -> none  [the longest x2 2.67 us: attend(): value_heads = value_rows.reshape(count, -1, HD)]
    reduce_sum x1 -> x0, other arithmetic: 4.02 us -> none  [add_sources(): return jnp.sum(received.astype(jnp.float32), axis=0)]
  transfers between devices with their start and end apart: 2 -> 0, of which waited for: 2 -> 0; matrix products, arithmetic and copies ran while one was open for 0% -> 0% of each run, Pallas kernels for 0% -> 0%
where the time goes in v1:
time: 63 us; the launch traced here: 62.6 us
  Pallas kernels  52.2 us (83%)
  local copies, waits for them, and re-layouts  10.4 us (17%)
    pallas_call x1, Pallas kernels, local(): pl.pallas_call(kernel, out_shape=jax.ShapeDtypeStruct((1, mine, width), B...  52.2 us
    unnamed x21, local copies, waits for them, and re-layouts  10.4 us

profile of v1, /device:TPU:1, one launch (start us, length us, event | category | flops | bytes accessed | tf_op | source)
XLA Modules:
  0.0 62.6 jit_solution(2273689436763990265)
XLA Ops:
  0.0 0.0 copy-start
  0.0 1.9 %copy-done = bf16[1,256,6144]{2,1,0:T(8,128)(2,1)S(1)} copy-done((bf16[1,256,6144]{2,1,0:T(8,128)(2,1)S(1)}, bf16[1,256,6144]{2,1,0:T(8,128)(2,1)}, u32[]{:S(2)}) %copy-start) | copy-done | bytes 3145752
  1.9 0.0 copy-start.1
  1.9 0.9 %copy-done.1 = bf16[1,16,6144]{2,1,0:T(8,128)(2,1)S(1)} copy-done((bf16[1,16,6144]{2,1,0:T(8,128)(2,1)S(1)}, bf16[1,16,6144]{2,1,0:T(8,128)(2,1)}, u32[]{:S(2)}) %copy-start.1) | copy-done | bytes 196632
  2.8 0.0 copy-start.2
  2.8 0.9 %copy-done.2 = bf16[1,256,256]{2,1,0:T(8,128)(2,1)S(1)} copy-done((bf16[1,256,256]{2,1,0:T(8,128)(2,1)S(1)}, bf16[1,256,256]{2,1,0:T(8,128)(2,1)}, u32[]{:S(2)}) %copy-start.2) | copy-done | bytes 131096
  3.7 0.0 copy-start.3
  3.7 0.9 %copy-done.3 = bf16[1,256,256]{2,1,0:T(8,128)(2,1)S(1)} copy-done((bf16[1,256,256]{2,1,0:T(8,128)(2,1)S(1)}, bf16[1,256,256]{2,1,0:T(8,128)(2,1)}, u32[]{:S(2)}) %copy-start.3) | copy-done | bytes 131096
  4.6 0.0 copy-start.4
  4.6 0.9 %copy-done.4 = bf16[1,256,256]{2,1,0:T(8,128)(2,1)S(1)} copy-done((bf16[1,256,256]{2,1,0:T(8,128)(2,1)S(1)}, bf16[1,256,256]{2,1,0:T(8,128)(2,1)}, u32[]{:S(2)}) %copy-start.4) | copy-done | bytes 131096
  5.5 0.0 copy-start.5
  5.5 0.9 %copy-done.5 = bf16[1,256,256]{2,1,0:T(8,128)(2,1)S(1)} copy-done((bf16[1,256,256]{2,1,0:T(8,128)(2,1)S(1)}, bf16[1,256,256]{2,1,0:T(8,128)(2,1)}, u32[]{:S(2)}) %copy-start.5) | copy-done | bytes 131096
  6.4 0.0 copy-start.6
  6.4 0.9 %copy-done.6 = bf16[1,256,256]{2,1,0:T(8,128)(2,1)S(1)} copy-done((bf16[1,256,256]{2,1,0:T(8,128)(2,1)S(1)}, bf16[1,256,256]{2,1,0:T(8,128)(2,1)}, u32[]{:S(2)}) %copy-start.6) | copy-done | bytes 131096
  7.3 0.0 copy-start.7
  7.3 0.9 %copy-done.7 = bf16[1,256,256]{2,1,0:T(8,128)(2,1)S(1)} copy-done((bf16[1,256,256]{2,1,0:T(8,128)(2,1)S(1)}, bf16[1,256,256]{2,1,0:T(8,128)(2,1)}, u32[]{:S(2)}) %copy-start.7) | copy-done | bytes 131096
  8.2 0.0 copy-start.8
  8.2 0.7 %copy-done.8 = f32[1,6144]{1,0:T(1,128)S(1)} copy-done((f32[1,6144]{1,0:T(1,128)S(1)}, f32[1,6144]{1,0:T(1,128)}, u32[]{:S(2)}) %copy-start.8) | copy-done | bytes 24600
  9.0 0.0 copy-start.9
  9.0 0.7 %copy-done.9 = s32[6144]{0:T(1024)S(1)} copy-done((s32[6144]{0:T(1024)S(1)}, s32[6144]{0:T(1024)}, u32[]{:S(2)}) %copy-start.9) | copy-done | bytes 24600
  9.7 52.2 %shard_map.100 = bf16[1,16,6144]{2,1,0:T(8,128)(2,1)S(1)} custom-call(bf16[1,256,256]{2,1,0:T(8,128)(2,1)S(1)} %copy-done.2, bf16[1,256,256]{2,1,0:T(8,128)(2,1)S(1)} %copy-done.3, bf16[1,256,256]{2,1,0:T(8,128)(2,1)S(1)} %copy-done.4, bf16[1,256,256]{2,1,0:T(8,128)(2,1)S(1)} %copy-done.5, bf16[1,256,256]{2,1,0:T(8,128)(2,1)S(1)} %copy-done.6, ...), custom_call_target="tpu_custom_call" | custom-call | flops 1610612736 | bytes 3145728 | tf_op jit(solution)/shard_map/pallas_call | solution.py:368
  61.9 0.7 %copy.12 = bf16[1,16,6144]{2,1,0:T(8,128)(2,1)} copy(bf16[1,16,6144]{2,1,0:T(8,128)(2,1)S(1)} %shard_map.100) | data formatting | bytes 393216
Async XLA Ops:
  0.0 1.9 %copy-start = (bf16[1,256,6144]{2,1,0:T(8,128)(2,1)S(1)}, bf16[1,256,6144]{2,1,0:T(8,128)(2,1)}, u32[]{:S(2)}) copy-start(bf16[1,256,6144]{2,1,0:T(8,128)(2,1)} %weight.1) | copy-start | bytes 9437188
  1.9 0.9 %copy-start.1 = (bf16[1,16,6144]{2,1,0:T(8,128)(2,1)S(1)}, bf16[1,16,6144]{2,1,0:T(8,128)(2,1)}, u32[]{:S(2)}) copy-start(bf16[1,16,6144]{2,1,0:T(8,128)(2,1)} %residual.1) | copy-start | bytes 589828
  2.8 0.9 %copy-start.2 = (bf16[1,256,256]{2,1,0:T(8,128)(2,1)S(1)}, bf16[1,256,256]{2,1,0:T(8,128)(2,1)}, u32[]{:S(2)}) copy-start(bf16[1,256,256]{2,1,0:T(8,128)(2,1)} %lq.1) | copy-start | bytes 393220
  3.7 0.9 %copy-start.3 = (bf16[1,256,256]{2,1,0:T(8,128)(2,1)S(1)}, bf16[1,256,256]{2,1,0:T(8,128)(2,1)}, u32[]{:S(2)}) copy-start(bf16[1,256,256]{2,1,0:T(8,128)(2,1)} %lk.1) | copy-start | bytes 393220
  4.6 0.9 %copy-start.4 = (bf16[1,256,256]{2,1,0:T(8,128)(2,1)S(1)}, bf16[1,256,256]{2,1,0:T(8,128)(2,1)}, u32[]{:S(2)}) copy-start(bf16[1,256,256]{2,1,0:T(8,128)(2,1)} %lv.1) | copy-start | bytes 393220
  5.5 0.9 %copy-start.5 = (bf16[1,256,256]{2,1,0:T(8,128)(2,1)S(1)}, bf16[1,256,256]{2,1,0:T(8,128)(2,1)}, u32[]{:S(2)}) copy-start(bf16[1,256,256]{2,1,0:T(8,128)(2,1)} %aq.1) | copy-start | bytes 393220
  6.4 0.9 %copy-start.6 = (bf16[1,256,256]{2,1,0:T(8,128)(2,1)S(1)}, bf16[1,256,256]{2,1,0:T(8,128)(2,1)}, u32[]{:S(2)}) copy-start(bf16[1,256,256]{2,1,0:T(8,128)(2,1)} %ak.1) | copy-start | bytes 393220
  7.3 0.9 %copy-start.7 = (bf16[1,256,256]{2,1,0:T(8,128)(2,1)S(1)}, bf16[1,256,256]{2,1,0:T(8,128)(2,1)}, u32[]{:S(2)}) copy-start(bf16[1,256,256]{2,1,0:T(8,128)(2,1)} %av.1) | copy-start | bytes 393220
  8.2 0.7 %copy-start.8 = (f32[1,6144]{1,0:T(1,128)S(1)}, f32[1,6144]{1,0:T(1,128)}, u32[]{:S(2)}) copy-start(f32[1,6144]{1,0:T(1,128)} %gate.1) | copy-start | bytes 73732
  9.0 0.7 %copy-start.9 = (s32[6144]{0:T(1024)S(1)}, s32[6144]{0:T(1024)}, u32[]{:S(2)}) copy-start(s32[6144]{0:T(1024)} %param.19) | copy-start | bytes 73732

commit v2 on v1

v2 whole, which is shorter than its diff:
```python
import math

import jax
import jax.numpy as jnp
from jax import lax
from jax.experimental import pallas as pl
from jax.experimental.pallas import tpu as pltpu
from jax.sharding import PartitionSpec as P

HD = 128
BLK = 128
MESH = pl.DeviceIdType.MESH
F32 = jnp.float32
BF16 = jnp.bfloat16
WIDTHS = (1024, 1024, 1024)
FIRST = (4, 3)
MODES = (
    (("next", "next", "apart", "apart"), ("next", "back", "back")),
    (("next", "next", "apart", "apart"), ("next", "back", "back")),
    (("next", "next", "apart", "apart"), ("next", "back", "back")),
)
ORDER = (
    ("P", 2), ("A4", 2), ("cB3", 2), ("P", 1), ("cA1", 1), ("cB3", 1), ("A4", 1), ("cA1", 2), ("P", 0), ("A4", 0),
    ("cA1", 0), ("cB3", 0), ("cB2", 1), ("cO", 0), ("cO", 2), ("A3", 2), ("jB3", 2), ("cB2", 0), ("cB2", 2),
    ("cO", 1), ("jB3", 1), ("A3", 1), ("A3", 0), ("jB3", 0), ("cA2", 2), ("jO", 0), ("jB2", 1), ("jO", 2),
    ("cA2", 1), ("jB2", 2), ("jO", 1), ("cA2", 0), ("jB2", 0), ("jA2", 2), ("cB1", 1), ("cB1", 2), ("jA2", 1),
    ("jA2", 0), ("cB1", 0), ("jA1", 2), ("jB1", 1), ("jA1", 1), ("jB1", 2), ("jA1", 0), ("jB1", 0), ("F", 1),
    ("F", 2), ("F", 0),
)
PIECES = len(WIDTHS)
STARTS = tuple(sum(WIDTHS[:p]) for p in range(PIECES))


def mode(ch, j, p):
    return MODES[p][ch][j - 1]


def joints(p):
    return [(ch, j) for ch, first in enumerate(FIRST) for j in range(1, first + 1) if mode(ch, j, p) != "apart"]


def kernel(
    lq, lk, lv, aq, ak, av, residual, weight, gate, sign_bits,
    out,
    qkv, qkv_sem,
    wbuf, w_sem, w_send, w_recv,
    att, att_send, att_recv,
    resbuf, res_sem, res_send, res_recv,
    table, signs, gates, gate_sem, sign_sem, bits_v,
    sums,
    zs, zr, zs_sem, zr_sem,
    xs, xr, xs_sem, xr_sem,
    fin, fs_sem, fin_sem,
    own0, own_keep, own_s, own_r, os_sem, or_sem,
):
    sections = lax.axis_size("section")
    chips = lax.axis_size("tp") // 2
    s = lax.axis_index("section")
    tp = lax.axis_index("tp")
    z = tp >> 1
    c = tp & 1
    other = 1 - c
    tokens = lq.shape[1]
    kd = lq.shape[2]
    width = residual.shape[2]
    half = width // 2
    rows = tokens // chips
    mine = rows // 2

    def wrapped(at, count):
        return jnp.where(at < 0, at + count, jnp.where(at >= count, at - count, at))

    side = 1 - 2 * c
    around = {k: wrapped(z + k * side, chips) for k in range(-max(FIRST), max(FIRST) + 1)}
    row_of = {k: pl.multiple_of(rows * at, rows) for k, at in around.items()}
    near = {k: {"section": s, "tp": 2 * around[k] + c} for k in (-1, 1)}
    near_core = {(k, core): {"section": s, "tp": 2 * around[k] + core} for k in (-1, 1) for core in (0, 1)}
    next_section = {"section": wrapped(s + 1, sections), "tp": tp}
    prev_section = {"section": wrapped(s - 1, sections), "tp": tp}
    partner = {"section": s, "tp": 2 * z + other}

    barrier = pltpu.get_barrier_semaphore()
    greeted = [partner, next_section, prev_section] + list(near_core.values())
    for device in greeted:
        pl.semaphore_signal(barrier, inc=1, device_id=device, device_id_type=MESH)

    def toward(ch, p):
        return 1 if (ch + p) % 2 == 0 else -1

    def cols(p, which):
        return pl.ds(pl.multiple_of(which * half + STARTS[p], 128), WIDTHS[p])

    loads = []
    for i, ref in enumerate((lq, lk, lv, aq, ak, av)):
        loads.append(pltpu.make_async_copy(ref.at[0], qkv.at[i], qkv_sem.at[i]))
        loads[-1].start()

    def w_local(p):
        return pltpu.make_async_copy(weight.at[0, :, cols(p, c)], wbuf[p].at[pl.ds(0, kd)], w_sem.at[p])

    def w_remote(p):
        return pltpu.make_async_remote_copy(
            weight.at[0, :, cols(p, other)], wbuf[p].at[pl.ds(kd, kd)], w_send.at[p], w_recv.at[p],
            device_id=partner, device_id_type=MESH)

    for p in range(PIECES):
        w_local(p).start()
    gate_copy = pltpu.make_async_copy(gate, gates, gate_sem)
    gate_copy.start()
    sign_copy = pltpu.make_async_copy(sign_bits, bits_v, sign_sem)
    sign_copy.start()
    own_rows = pl.ds(pl.multiple_of(mine * c, mine), mine)
    other_rows = pl.ds(pl.multiple_of(mine * other, mine), mine)
    res_local = pltpu.make_async_copy(
        residual.at[0, :, pl.ds(pl.multiple_of(c * half, 128), half)], resbuf.at[own_rows], res_sem)
    res_local.start()

    pl.semaphore_wait(barrier, len(greeted))

    for p in range(PIECES):
        w_remote(p).start()
    res_remote = pltpu.make_async_remote_copy(
        residual.at[0, :, pl.ds(pl.multiple_of(other * half, 128), half)], resbuf.at[own_rows], res_send, res_recv,
        device_id=partner, device_id_type=MESH)
    res_remote.start()

    def att_copy(m):
        there = att.at[pl.ds(m * tokens, tokens), pl.ds(kd, kd)]
        here = att.at[pl.ds(m * tokens, tokens), pl.ds(0, kd)]
        return pltpu.make_async_remote_copy(
            here, there, att_send.at[m], att_recv.at[m], device_id=partner, device_id_type=MESH)

    for m in range(2):
        for i in range(3):
            loads[3 * m + i].wait()
        for h in range(kd // HD):
            lanes = pl.ds(h * HD, HD)
            query, key, value = (qkv[3 * m + i, :, lanes] for i in range(3))
            scores = lax.dot_general(query, key, (((1,), (1,)), ((), ())), preferred_element_type=F32)
            scores = scores * (1.0 / math.sqrt(HD))
            peak = jnp.max(scores, axis=-1, keepdims=True)
            raised = jnp.exp(scores - peak)
            probs = (raised / jnp.sum(raised, axis=-1, keepdims=True)).astype(BF16)
            mixed = jnp.dot(probs, value, preferred_element_type=F32)
            att[pl.ds(m * tokens, tokens), lanes] = mixed.astype(BF16)
        att_copy(m).start()

    i = lax.broadcasted_iota(jnp.int32, (BLK, BLK), 0)
    j = lax.broadcasted_iota(jnp.int32, (BLK, BLK), 1)
    anded = i & j
    anded = anded ^ (anded >> 4)
    anded = anded ^ (anded >> 2)
    anded = anded ^ (anded >> 1)
    table[...] = (1 - 2 * (anded & 1)).astype(F32).astype(BF16)
    sign_copy.wait()
    signs[...] = 1.0 - 2.0 * bits_v[...].astype(F32)

    def turned(values):
        r, n = values.shape[0], values.shape[1] // BLK
        blocks = jnp.concatenate([values[:, b * BLK:(b + 1) * BLK] for b in range(n)], axis=0)
        made = jnp.dot(blocks, table[...], preferred_element_type=F32)
        return jnp.concatenate([made[b * r:(b + 1) * r] for b in range(n)], axis=1)

    gate_copy.wait()
    res_local.wait()
    res_remote.wait_recv()
    for m in range(2):
        att_copy(m).wait_recv()

    def leaving(p, at):
        return sums[p][pl.ds(row_of[at], rows), :]

    def arriving(p, at):
        return sums[p][pl.ds(pl.multiple_of(tokens + row_of[at], rows), rows), :]

    def z_copy(ch, j, p):
        to = near[toward(ch, p)]
        return pltpu.make_async_remote_copy(
            zs[p][ch][j], zr[p][ch][j], zs_sem.at[ch, j, p], zr_sem.at[ch, j, p], device_id=to, device_id_type=MESH)

    def fin_copy(ch, core, p):
        to = near_core[toward(ch, p), core]
        return pltpu.make_async_remote_copy(
            zs[p][ch][1].at[pl.ds(core * mine, mine)], fin[p].at[ch, c],
            fs_sem.at[ch, core, p], fin_sem.at[ch, c, p], device_id=to, device_id_type=MESH)

    def fin_arrival(ch, core, p):
        return pltpu.make_async_remote_copy(
            zs[p][ch][1].at[pl.ds(0, mine)], fin[p].at[ch, core],
            fs_sem.at[ch, 0, p], fin_sem.at[ch, core, p], device_id=partner, device_id_type=MESH)

    def x_copy(at, p):
        to = next_section if at == 0 or mode(*joints(p)[at - 1], p) == "next" else prev_section
        return pltpu.make_async_remote_copy(
            xs[p].at[at], xr[p].at[at], xs_sem.at[at, p], xr_sem.at[at, p], device_id=to, device_id_type=MESH)

    def slot(ch, j, p):
        return joints(p).index((ch, j)) + 1

    def own_copy(p):
        return pltpu.make_async_remote_copy(
            own_s[p], own_r[p], os_sem.at[p], or_sem.at[p], device_id=partner, device_id_type=MESH)

    def target(ch, j, p):
        return j * toward(ch, p)

    def come(ch, j, p, arrived):
        kind = mode(ch, j + 1, p) if j < FIRST[ch] else None
        if kind == "apart":
            return zr[p][ch][j + 1][rows:] if arrived else zr[p][ch][j + 1][:rows]
        if kind == ("next" if arrived else "back"):
            return zr[p][ch][j + 1][...]
        return None

    def plus(sums_here, other_sums):
        return sums_here if other_sums is None else sums_here + other_sums.astype(F32)

    def apart(ch, j, p):
        if j < FIRST[ch]:
            z_copy(ch, j + 1, p).wait_recv()
        at = target(ch, j, p)
        zs[p][ch][j][:rows] = plus(leaving(p, at), come(ch, j, p, False)).astype(BF16)
        zs[p][ch][j][rows:] = plus(arriving(p, at), come(ch, j, p, True)).astype(BF16)
        z_copy(ch, j, p).start()

    def cross(ch, j, p):
        arrived = mode(ch, j, p) == "back"
        own = (arriving if arrived else leaving)(p, target(ch, j, p))
        if come(ch, j, p, arrived) is not None:
            z_copy(ch, j + 1, p).wait_recv()
        xs[p][slot(ch, j, p)] = plus(own, come(ch, j, p, arrived)).astype(BF16)
        x_copy(slot(ch, j, p), p).start()

    def joined(ch, j, p):
        arrived = mode(ch, j, p) == "next"
        own = (arriving if arrived else leaving)(p, target(ch, j, p))
        x_copy(slot(ch, j, p), p).wait_recv()
        own = own + xr[p][slot(ch, j, p)].astype(F32)
        if come(ch, j, p, arrived) is not None and come(ch, j, p, not arrived) is None:
            z_copy(ch, j + 1, p).wait_recv()
        zs[p][ch][j][...] = plus(own, come(ch, j, p, arrived)).astype(BF16)
        if j > 1:
            z_copy(ch, j, p).start()
        else:
            for core in (0, 1):
                fin_copy(ch, core, p).start()

    def own_cross(p):
        plain = turned(resbuf[:, pl.ds(STARTS[p], WIDTHS[p])])
        plain = plain * (signs[:, cols(p, c)] * (1.0 / math.sqrt(BLK)))
        xs[p][0] = (leaving(p, 0) + plain).astype(BF16)
        x_copy(0, p).start()

    def own_joined(p):
        x_copy(0, p).wait_recv()
        own0[p][...] = arriving(p, 0) + xr[p][0].astype(F32)
        own_keep[p][...] = own0[p][own_rows, :]
        own_s[p][...] = own0[p][other_rows, :].astype(BF16)
        own_copy(p).start()

    def project(p):
        w_local(p).wait()
        w_remote(p).wait_recv()
        made = jnp.dot(att[...], wbuf[p][...], preferred_element_type=F32)
        sums[p][...] = made * gates[:, cols(p, c)]

    def finish(p):
        w_remote(p).wait_send()
        for at in range(1 + len(joints(p))):
            x_copy(at, p).wait_send()
        for ch, first in enumerate(FIRST):
            for j in range(2, first + 1):
                z_copy(ch, j, p).wait_send()
        own_copy(p).wait()
        for ch in range(2):
            for core in (0, 1):
                fin_copy(ch, core, p).wait_send()
                fin_arrival(ch, core, p).wait_recv()
        for core, own in ((c, own_keep[p][...]), (other, own_r[p][...].astype(F32))):
            total = own + fin[p][0, core].astype(F32) + fin[p][1, core].astype(F32)
            total = total * signs[:, cols(p, core)]
            high = total.astype(BF16)
            low = (total - high.astype(F32)).astype(BF16)
            r = turned(jnp.concatenate([high, low], axis=0))
            r = (r[:mine] + r[mine:]) * (1.0 / math.sqrt(BLK))
            out[0, :, cols(p, core)] = r.astype(BF16)

    for step, p in ORDER:
        if step == "P":
            project(p)
        elif step == "F":
            finish(p)
        elif step == "cO":
            own_cross(p)
        elif step == "jO":
            own_joined(p)
        else:
            ch, j = "AB".index(step[-2]), int(step[-1])
            (cross if step[0] == "c" else joined if step[0] == "j" else apart)(ch, j, p)

    res_remote.wait_send()
    for m in range(2):
        att_copy(m).wait_send()


def local(
    leave_query, leave_key, leave_value, arrive_query, arrive_key, arrive_value,
    leave_residual, out_weight, gate_scale, sign_bits,
):
    tokens, kd = leave_query.shape[1:]
    width = leave_residual.shape[2]
    chips = lax.axis_size("tp") // 2
    rows, mine = tokens // chips, tokens // chips // 2
    half = width // 2
    dma = pltpu.SemaphoreType.DMA

    def each(shape, kind):
        return [pltpu.VMEM(shape + (w,), kind) for w in WIDTHS]

    def hops():
        return [
            [[pltpu.VMEM((2 * rows if j > 0 and mode(ch, j, p) == "apart" else rows, w), BF16) for j in range(first + 1)]
             for ch, first in enumerate(FIRST)]
            for p, w in enumerate(WIDTHS)
        ]

    def crossings():
        return [pltpu.VMEM((1 + len(joints(p)), rows, w), BF16) for p, w in enumerate(WIDTHS)]

    most = max(FIRST) + 1
    nx = 1 + max(len(joints(p)) for p in range(PIECES))
    scratch = [
        pltpu.VMEM((6, tokens, kd), BF16), dma((6,)),
        each((2 * kd,), BF16), dma((PIECES,)), dma((PIECES,)), dma((PIECES,)),
        pltpu.VMEM((2 * tokens, 2 * kd), BF16), dma((2,)), dma((2,)),
        pltpu.VMEM((rows, half), BF16), dma, dma, dma,
        pltpu.VMEM((BLK, BLK), BF16), pltpu.VMEM((1, width), F32), pltpu.VMEM((1, width), F32), dma, dma,
        pltpu.VMEM((1, width), jnp.int32),
        each((2 * tokens,), F32),
        hops(), hops(), dma((2, most, PIECES)), dma((2, most, PIECES)),
        crossings(), crossings(), dma((nx, PIECES)), dma((nx, PIECES)),
        each((2, 2, mine), BF16), dma((2, 2, PIECES)), dma((2, 2, PIECES)),
        each((rows,), F32), each((mine,), F32), each((mine,), BF16), each((mine,), BF16),
        dma((PIECES,)), dma((PIECES,)),
    ]
    operands = (
        leave_query, leave_key, leave_value, arrive_query, arrive_key, arrive_value,
        leave_residual, out_weight, gate_scale, sign_bits.reshape(1, width),
    )
    return pl.pallas_call(
        kernel,
        out_shape=pltpu.VMEM((1, mine, width), BF16),
        in_specs=[pl.BlockSpec(memory_space=pltpu.HBM)] * len(operands),
        out_specs=pl.BlockSpec(memory_space=pltpu.VMEM),
        scratch_shapes=scratch,
        compiler_params=pltpu.CompilerParams(
            collective_id=0, has_side_effects=True, vmem_limit_bytes=48 * 1024 * 1024),
        cost_estimate=pl.CostEstimate(
            flops=2 * 2 * tokens * kd * width, bytes_accessed=2 * kd * width, transcendentals=0),
    )(*(pltpu.with_memory_space_constraint(x, pltpu.HBM) for x in operands))


def solution(mesh):
    placed = (
        P("section", None, "tp"),
        P("section", None, "tp"),
        P("section", None, "tp"),
        P("section", None, "tp"),
        P("section", None, "tp"),
        P("section", None, "tp"),
        P("section", "tp", None),
        P("section", "tp", None),
        P("section", None),
        P(),
    )
    return jax.shard_map(
        local, mesh=mesh, in_specs=placed, out_specs=P("section", "tp", None), check_vma=False
    )
```

time: 63 us -> 47.6 us (0.76)
  local copies, waits for them, and re-layouts: 10.4 us -> 0.68 us
  Pallas kernels: 52.2 us -> 46.8 us
    unnamed x21 -> x1, local copies, waits for them, and re-layouts: 10.4 us -> 0.68 us
    pallas_call x1, Pallas kernels: 52.2 us -> 46.8 us  [local(): pl.pallas_call(kernel, out_shape=pltpu.VMEM((1, mine, width), BF16), in_s...]
where the time goes in v2:
time: 47.6 us; the launch traced here: 47.5 us
  Pallas kernels  46.8 us (98%)
  local copies, waits for them, and re-layouts  0.68 us (1%)
    pallas_call x1, Pallas kernels, local(): pl.pallas_call(kernel, out_shape=pltpu.VMEM((1, mine, width), BF16), in_s...  46.8 us

profile of v2, /device:TPU:1, one launch (start us, length us, event | category | flops | bytes accessed | tf_op | source)
XLA Modules:
  0.0 47.5 jit_solution(2791148325499572801)
XLA Ops:
  0.0 46.8 %shard_map.100 = bf16[1,16,6144]{2,1,0:T(8,128)(2,1)S(1)} custom-call(bf16[1,256,256]{2,1,0:T(8,128)(2,1)} %lq.1, bf16[1,256,256]{2,1,0:T(8,128)(2,1)} %lk.1, bf16[1,256,256]{2,1,0:T(8,128)(2,1)} %lv.1, bf16[1,256,256]{2,1,0:T(8,128)(2,1)} %aq.1, bf16[1,256,256]{2,1,0:T(8,128)(2,1)} %ak.1, bf16[1,256,256]{2,1,0:T(8,128)(2,1)} %av.1, ...), custom_call_target="tpu_custom_call" | custom-call | flops 1610612736 | bytes 3145728 | tf_op jit(solution)/shard_map/pallas_call | solution.py:350
  46.8 0.7 %copy.12 = bf16[1,16,6144]{2,1,0:T(8,128)(2,1)} copy(bf16[1,16,6144]{2,1,0:T(8,128)(2,1)S(1)} %shard_map.100) | data formatting | bytes 393216

commit v3 on v2

--- a/solution.py
+++ b/solution.py
@@ -12,7 +12,7 @@
 MESH = pl.DeviceIdType.MESH
 F32 = jnp.float32
 BF16 = jnp.bfloat16
-WIDTHS = (1024, 1024, 1024)
+WIDTHS = (768, 1280, 1024)
 FIRST = (4, 3)
 MODES = (
     (("next", "next", "apart", "apart"), ("next", "back", "back")),
@@ -20,12 +20,12 @@
     (("next", "next", "apart", "apart"), ("next", "back", "back")),
 )
 ORDER = (
-    ("P", 2), ("A4", 2), ("cB3", 2), ("P", 1), ("cA1", 1), ("cB3", 1), ("A4", 1), ("cA1", 2), ("P", 0), ("A4", 0),
-    ("cA1", 0), ("cB3", 0), ("cB2", 1), ("cO", 0), ("cO", 2), ("A3", 2), ("jB3", 2), ("cB2", 0), ("cB2", 2),
-    ("cO", 1), ("jB3", 1), ("A3", 1), ("A3", 0), ("jB3", 0), ("cA2", 2), ("jO", 0), ("jB2", 1), ("jO", 2),
-    ("cA2", 1), ("jB2", 2), ("jO", 1), ("cA2", 0), ("jB2", 0), ("jA2", 2), ("cB1", 1), ("cB1", 2), ("jA2", 1),
-    ("jA2", 0), ("cB1", 0), ("jA1", 2), ("jB1", 1), ("jA1", 1), ("jB1", 2), ("jA1", 0), ("jB1", 0), ("F", 1),
-    ("F", 2), ("F", 0),
+    ("P", 0), ("cB3", 0), ("A4", 0), ("cA1", 0), ("P", 1), ("A4", 1), ("cO", 0), ("P", 2), ("cB3", 1), ("A4", 2),
+    ("cA1", 2), ("cO", 1), ("cB2", 0), ("jB3", 0), ("cB3", 2), ("A3", 0), ("cA1", 1), ("cB2", 1), ("A3", 1),
+    ("jB3", 1), ("cO", 2), ("cB2", 2), ("A3", 2), ("jB3", 2), ("cA2", 0), ("jO", 0), ("jB2", 0), ("jO", 1),
+    ("cA2", 1), ("jB2", 1), ("cA2", 2), ("jB2", 2), ("cB1", 0), ("cB1", 1), ("jA2", 0), ("jA2", 1), ("jA2", 2),
+    ("jO", 2), ("cB1", 2), ("jB1", 0), ("jA1", 0), ("jA1", 1), ("jB1", 1), ("jA1", 2), ("jB1", 2), ("F", 0),
+    ("F", 1), ("F", 2),
 )
 PIECES = len(WIDTHS)
 STARTS = tuple(sum(WIDTHS[:p]) for p in range(PIECES))
@@ -43,7 +43,7 @@
     lq, lk, lv, aq, ak, av, residual, weight, gate, sign_bits,
     out,
     qkv, qkv_sem,
-    wbuf, w_sem, w_send, w_recv,
+    wbuf, w_sem, w_send, w_recv, wahead, ahead_sem,
     att, att_send, att_recv,
     resbuf, res_sem, res_send, res_recv,
     table, signs, gates, gate_sem, sign_sem, bits_v,
@@ -98,11 +98,20 @@
     def w_local(p):
         return pltpu.make_async_copy(weight.at[0, :, cols(p, c)], wbuf[p].at[pl.ds(0, kd)], w_sem.at[p])
 
+    def w_ahead(p):
+        return pltpu.make_async_copy(weight.at[0, :, cols(p, other)], wahead[p], ahead_sem.at[p])
+
+    def send_weights(p):
+        w_ahead(p).wait()
+        w_remote(p).start()
+
     def w_remote(p):
         return pltpu.make_async_remote_copy(
-            weight.at[0, :, cols(p, other)], wbuf[p].at[pl.ds(kd, kd)], w_send.at[p], w_recv.at[p],
+            wahead[p], wbuf[p].at[pl.ds(kd, kd)], w_send.at[p], w_recv.at[p],
             device_id=partner, device_id_type=MESH)
 
+    for p in range(PIECES):
+        w_ahead(p).start()
     for p in range(PIECES):
         w_local(p).start()
     gate_copy = pltpu.make_async_copy(gate, gates, gate_sem)
@@ -117,12 +126,11 @@
 
     pl.semaphore_wait(barrier, len(greeted))
 
-    for p in range(PIECES):
-        w_remote(p).start()
     res_remote = pltpu.make_async_remote_copy(
         residual.at[0, :, pl.ds(pl.multiple_of(other * half, 128), half)], resbuf.at[own_rows], res_send, res_recv,
         device_id=partner, device_id_type=MESH)
     res_remote.start()
+    send_weights(0)
 
     def att_copy(m):
         there = att.at[pl.ds(m * tokens, tokens), pl.ds(kd, kd)]
@@ -144,6 +152,8 @@
             mixed = jnp.dot(probs, value, preferred_element_type=F32)
             att[pl.ds(m * tokens, tokens), lanes] = mixed.astype(BF16)
         att_copy(m).start()
+    for p in range(1, PIECES):
+        send_weights(p)
 
     i = lax.broadcasted_iota(jnp.int32, (BLK, BLK), 0)
     j = lax.broadcasted_iota(jnp.int32, (BLK, BLK), 1)
@@ -162,8 +172,6 @@
         return jnp.concatenate([made[b * r:(b + 1) * r] for b in range(n)], axis=1)
 
     gate_copy.wait()
-    res_local.wait()
-    res_remote.wait_recv()
     for m in range(2):
         att_copy(m).wait_recv()
 
@@ -246,6 +254,9 @@
                 fin_copy(ch, core, p).start()
 
     def own_cross(p):
+        if p == ORDER[[step for step, _ in ORDER].index("cO")][1]:
+            res_local.wait()
+            res_remote.wait_recv()
         plain = turned(resbuf[:, pl.ds(STARTS[p], WIDTHS[p])])
         plain = plain * (signs[:, cols(p, c)] * (1.0 / math.sqrt(BLK)))
         xs[p][0] = (leaving(p, 0) + plain).astype(BF16)
@@ -331,7 +342,7 @@
     nx = 1 + max(len(joints(p)) for p in range(PIECES))
     scratch = [
         pltpu.VMEM((6, tokens, kd), BF16), dma((6,)),
-        each((2 * kd,), BF16), dma((PIECES,)), dma((PIECES,)), dma((PIECES,)),
+        each((2 * kd,), BF16), dma((PIECES,)), dma((PIECES,)), dma((PIECES,)), each((kd,), BF16), dma((PIECES,)),
         pltpu.VMEM((2 * tokens, 2 * kd), BF16), dma((2,)), dma((2,)),
         pltpu.VMEM((rows, half), BF16), dma, dma, dma,
         pltpu.VMEM((BLK, BLK), BF16), pltpu.VMEM((1, width), F32), pltpu.VMEM((1, width), F32), dma, dma,

time: 47.6 us -> 46.9 us (0.985)
  Pallas kernels: 46.8 us -> 46.1 us
    pallas_call x1, Pallas kernels: 46.8 us -> 46.1 us  [local(): pl.pallas_call(kernel, out_shape=pltpu.VMEM((1, mine, width), BF16), in_s...]
where the time goes in v3:
time: 46.9 us; the launch traced here: 46.8 us
  Pallas kernels  46.1 us (98%)
  local copies, waits for them, and re-layouts  0.68 us (1%)
    pallas_call x1, Pallas kernels, local(): pl.pallas_call(kernel, out_shape=pltpu.VMEM((1, mine, width), BF16), in_s...  46.1 us

profile of v3, /device:TPU:1, one launch (start us, length us, event | category | flops | bytes accessed | tf_op | source)
XLA Modules:
  0.0 46.8 jit_solution(9034157030078935518)
XLA Ops:
  0.0 46.1 %shard_map.100 = bf16[1,16,6144]{2,1,0:T(8,128)(2,1)S(1)} custom-call(bf16[1,256,256]{2,1,0:T(8,128)(2,1)} %lq.1, bf16[1,256,256]{2,1,0:T(8,128)(2,1)} %lk.1, bf16[1,256,256]{2,1,0:T(8,128)(2,1)} %lv.1, bf16[1,256,256]{2,1,0:T(8,128)(2,1)} %aq.1, bf16[1,256,256]{2,1,0:T(8,128)(2,1)} %ak.1, bf16[1,256,256]{2,1,0:T(8,128)(2,1)} %av.1, ...), custom_call_target="tpu_custom_call" | custom-call | flops 1610612736 | bytes 3145728 | tf_op jit(solution)/shard_map/pallas_call | solution.py:361
  46.1 0.7 %copy.12 = bf16[1,16,6144]{2,1,0:T(8,128)(2,1)} copy(bf16[1,16,6144]{2,1,0:T(8,128)(2,1)S(1)} %shard_map.100) | data formatting | bytes 393216

commit v4 on v3

--- a/solution.py
+++ b/solution.py
@@ -48,10 +48,10 @@
     resbuf, res_sem, res_send, res_recv,
     table, signs, gates, gate_sem, sign_sem, bits_v,
     sums,
-    zs, zr, zs_sem, zr_sem,
-    xs, xr, xs_sem, xr_sem,
-    fin, fs_sem, fin_sem,
-    own0, own_keep, own_s, own_r, os_sem, or_sem,
+    zs, zr, zr_sem,
+    xs, xr, xr_sem,
+    fin, fin_sem, sent,
+    own0, own_keep, own_s, own_r, or_sem,
 ):
     sections = lax.axis_size("section")
     chips = lax.axis_size("tp") // 2
@@ -172,8 +172,6 @@
         return jnp.concatenate([made[b * r:(b + 1) * r] for b in range(n)], axis=1)
 
     gate_copy.wait()
-    for m in range(2):
-        att_copy(m).wait_recv()
 
     def leaving(p, at):
         return sums[p][pl.ds(row_of[at], rows), :]
@@ -184,30 +182,30 @@
     def z_copy(ch, j, p):
         to = near[toward(ch, p)]
         return pltpu.make_async_remote_copy(
-            zs[p][ch][j], zr[p][ch][j], zs_sem.at[ch, j, p], zr_sem.at[ch, j, p], device_id=to, device_id_type=MESH)
+            zs[p][ch][j], zr[p][ch][j], sent.at[p], zr_sem.at[ch, j, p], device_id=to, device_id_type=MESH)
 
     def fin_copy(ch, core, p):
         to = near_core[toward(ch, p), core]
         return pltpu.make_async_remote_copy(
             zs[p][ch][1].at[pl.ds(core * mine, mine)], fin[p].at[ch, c],
-            fs_sem.at[ch, core, p], fin_sem.at[ch, c, p], device_id=to, device_id_type=MESH)
+            sent.at[p], fin_sem.at[ch, c, p], device_id=to, device_id_type=MESH)
 
     def fin_arrival(ch, core, p):
         return pltpu.make_async_remote_copy(
             zs[p][ch][1].at[pl.ds(0, mine)], fin[p].at[ch, core],
-            fs_sem.at[ch, 0, p], fin_sem.at[ch, core, p], device_id=partner, device_id_type=MESH)
+            sent.at[p], fin_sem.at[ch, core, p], device_id=partner, device_id_type=MESH)
 
     def x_copy(at, p):
         to = next_section if at == 0 or mode(*joints(p)[at - 1], p) == "next" else prev_section
         return pltpu.make_async_remote_copy(
-            xs[p].at[at], xr[p].at[at], xs_sem.at[at, p], xr_sem.at[at, p], device_id=to, device_id_type=MESH)
+            xs[p].at[at], xr[p].at[at], sent.at[p], xr_sem.at[at, p], device_id=to, device_id_type=MESH)
 
     def slot(ch, j, p):
         return joints(p).index((ch, j)) + 1
 
     def own_copy(p):
         return pltpu.make_async_remote_copy(
-            own_s[p], own_r[p], os_sem.at[p], or_sem.at[p], device_id=partner, device_id_type=MESH)
+            own_s[p], own_r[p], sent.at[p], or_sem.at[p], device_id=partner, device_id_type=MESH)
 
     def target(ch, j, p):
         return j * toward(ch, p)
@@ -270,22 +268,24 @@
         own_copy(p).start()
 
     def project(p):
+        if p > 0:
+            w_local(p).wait()
+            w_remote(p).wait_recv()
+            made = jnp.dot(att[...], wbuf[p][...], preferred_element_type=F32)
+            sums[p][...] = made * gates[:, cols(p, c)]
+            return
         w_local(p).wait()
+        sums[p][...] = jnp.dot(att[:, :kd], wbuf[p][:kd], preferred_element_type=F32)
+        for m in range(2):
+            att_copy(m).wait_recv()
         w_remote(p).wait_recv()
-        made = jnp.dot(att[...], wbuf[p][...], preferred_element_type=F32)
+        made = sums[p][...] + jnp.dot(att[:, kd:], wbuf[p][kd:], preferred_element_type=F32)
         sums[p][...] = made * gates[:, cols(p, c)]
 
     def finish(p):
-        w_remote(p).wait_send()
-        for at in range(1 + len(joints(p))):
-            x_copy(at, p).wait_send()
-        for ch, first in enumerate(FIRST):
-            for j in range(2, first + 1):
-                z_copy(ch, j, p).wait_send()
-        own_copy(p).wait()
+        own_copy(p).wait_recv()
         for ch in range(2):
             for core in (0, 1):
-                fin_copy(ch, core, p).wait_send()
                 fin_arrival(ch, core, p).wait_recv()
         for core, own in ((c, own_keep[p][...]), (other, own_r[p][...].astype(F32))):
             total = own + fin[p][0, core].astype(F32) + fin[p][1, core].astype(F32)
@@ -312,6 +312,13 @@
     res_remote.wait_send()
     for m in range(2):
         att_copy(m).wait_send()
+    for p in range(PIECES):
+        w_remote(p).wait_send()
+        count = mine + rows * (1 + len(joints(p)) + len(FIRST))
+        for ch, first in enumerate(FIRST):
+            count += sum(zs[p][ch][j].shape[0] for j in range(2, first + 1))
+        whole = wbuf[p].at[pl.ds(0, count)]
+        pltpu.make_async_copy(whole, whole, sent.at[p]).wait()
 
 
 def local(
@@ -348,11 +355,11 @@
         pltpu.VMEM((BLK, BLK), BF16), pltpu.VMEM((1, width), F32), pltpu.VMEM((1, width), F32), dma, dma,
         pltpu.VMEM((1, width), jnp.int32),
         each((2 * tokens,), F32),
-        hops(), hops(), dma((2, most, PIECES)), dma((2, most, PIECES)),
-        crossings(), crossings(), dma((nx, PIECES)), dma((nx, PIECES)),
-        each((2, 2, mine), BF16), dma((2, 2, PIECES)), dma((2, 2, PIECES)),
+        hops(), hops(), dma((2, most, PIECES)),
+        crossings(), crossings(), dma((nx, PIECES)),
+        each((2, 2, mine), BF16), dma((2, 2, PIECES)), dma((PIECES,)),
         each((rows,), F32), each((mine,), F32), each((mine,), BF16), each((mine,), BF16),
-        dma((PIECES,)), dma((PIECES,)),
+        dma((PIECES,)),
     ]
     operands = (
         leave_query, leave_key, leave_value, arrive_query, arrive_key, arrive_value,

time: 46.9 us -> 46.4 us (0.989)
  Pallas kernels: 46.1 us -> 45.6 us
    pallas_call x1, Pallas kernels: 46.1 us -> 45.6 us  [local(): pl.pallas_call(kernel, out_shape=pltpu.VMEM((1, mine, width), BF16), in_s...]
where the time goes in v4:
time: 46.4 us; the launch traced here: 46.3 us
  Pallas kernels  45.6 us (98%)
  local copies, waits for them, and re-layouts  0.68 us (1%)
    pallas_call x1, Pallas kernels, local(): pl.pallas_call(kernel, out_shape=pltpu.VMEM((1, mine, width), BF16), in_s...  45.6 us

profile of v4, /device:TPU:1, one launch (start us, length us, event | category | flops | bytes accessed | tf_op | source)
XLA Modules:
  0.0 46.3 jit_solution(13896897810218220967)
XLA Ops:
  0.0 45.6 %shard_map.100 = bf16[1,16,6144]{2,1,0:T(8,128)(2,1)S(1)} custom-call(bf16[1,256,256]{2,1,0:T(8,128)(2,1)} %lq.1, bf16[1,256,256]{2,1,0:T(8,128)(2,1)} %lk.1, bf16[1,256,256]{2,1,0:T(8,128)(2,1)} %lv.1, bf16[1,256,256]{2,1,0:T(8,128)(2,1)} %aq.1, bf16[1,256,256]{2,1,0:T(8,128)(2,1)} %ak.1, bf16[1,256,256]{2,1,0:T(8,128)(2,1)} %av.1, ...), custom_call_target="tpu_custom_call" | custom-call | flops 1610612736 | bytes 3145728 | tf_op jit(solution)/shard_map/pallas_call | solution.py:368
  45.6 0.7 %copy.12 = bf16[1,16,6144]{2,1,0:T(8,128)(2,1)} copy(bf16[1,16,6144]{2,1,0:T(8,128)(2,1)S(1)} %shard_map.100) | data formatting | bytes 393216

commit v5 on v4

--- a/solution.py
+++ b/solution.py
@@ -188,12 +188,11 @@
         to = near_core[toward(ch, p), core]
         return pltpu.make_async_remote_copy(
             zs[p][ch][1].at[pl.ds(core * mine, mine)], fin[p].at[ch, c],
-            sent.at[p], fin_sem.at[ch, c, p], device_id=to, device_id_type=MESH)
-
-    def fin_arrival(ch, core, p):
-        return pltpu.make_async_remote_copy(
-            zs[p][ch][1].at[pl.ds(0, mine)], fin[p].at[ch, core],
-            sent.at[p], fin_sem.at[ch, core, p], device_id=partner, device_id_type=MESH)
+            sent.at[p], fin_sem.at[p], device_id=to, device_id_type=MESH)
+
+    def fin_arrivals(p):
+        whole = wbuf[p].at[pl.ds(0, 4 * mine)]
+        return pltpu.make_async_copy(whole, whole, fin_sem.at[p])
 
     def x_copy(at, p):
         to = next_section if at == 0 or mode(*joints(p)[at - 1], p) == "next" else prev_section
@@ -284,9 +283,7 @@
 
     def finish(p):
         own_copy(p).wait_recv()
-        for ch in range(2):
-            for core in (0, 1):
-                fin_arrival(ch, core, p).wait_recv()
+        fin_arrivals(p).wait()
         for core, own in ((c, own_keep[p][...]), (other, own_r[p][...].astype(F32))):
             total = own + fin[p][0, core].astype(F32) + fin[p][1, core].astype(F32)
             total = total * signs[:, cols(p, core)]
@@ -357,7 +354,7 @@
         each((2 * tokens,), F32),
         hops(), hops(), dma((2, most, PIECES)),
         crossings(), crossings(), dma((nx, PIECES)),
-        each((2, 2, mine), BF16), dma((2, 2, PIECES)), dma((PIECES,)),
+        each((2, 2, mine), BF16), dma((PIECES,)), dma((PIECES,)),
         each((rows,), F32), each((mine,), F32), each((mine,), BF16), each((mine,), BF16),
         dma((PIECES,)),
     ]

time: 46.4 us -> 46.3 us (level)
  no operation moved by 1% of the time
where the time goes in v5:
time: 46.3 us; the launch traced here: 46.2 us
  Pallas kernels  45.5 us (98%)
  local copies, waits for them, and re-layouts  0.68 us (1%)
    pallas_call x1, Pallas kernels, local(): pl.pallas_call(kernel, out_shape=pltpu.VMEM((1, mine, width), BF16), in_s...  45.5 us

profile of v5, /device:TPU:1, one launch (start us, length us, event | category | flops | bytes accessed | tf_op | source)
XLA Modules:
  0.0 46.2 jit_solution(4142775830293291038)
XLA Ops:
  0.0 45.5 %shard_map.100 = bf16[1,16,6144]{2,1,0:T(8,128)(2,1)S(1)} custom-call(bf16[1,256,256]{2,1,0:T(8,128)(2,1)} %lq.1, bf16[1,256,256]{2,1,0:T(8,128)(2,1)} %lk.1, bf16[1,256,256]{2,1,0:T(8,128)(2,1)} %lv.1, bf16[1,256,256]{2,1,0:T(8,128)(2,1)} %aq.1, bf16[1,256,256]{2,1,0:T(8,128)(2,1)} %ak.1, bf16[1,256,256]{2,1,0:T(8,128)(2,1)} %av.1, ...), custom_call_target="tpu_custom_call" | custom-call | flops 1610612736 | bytes 3145728 | tf_op jit(solution)/shard_map/pallas_call | solution.py:365
  45.5 0.7 %copy.12 = bf16[1,16,6144]{2,1,0:T(8,128)(2,1)} copy(bf16[1,16,6144]{2,1,0:T(8,128)(2,1)S(1)} %shard_map.100) | data formatting | bytes 393216
